TPU v7x, 32 devices: a whole 2x2x4 slice. The times are simulated.
32 devices in a mesh: grp: 2 (over y), grid: 4 (over z), rep: 4 (over x, core).
Axes of the slice: x: 2, y: 2, z: 4, core: 2. Of those that a mesh axis runs over, the one named last changes fastest.
Arguments:
- task_blocks: float32 [48, 8, 128, 128], P(('grp', 'grid'), 'rep'), parts along dimension 0, may hold values from -1.75 to 1.75
- block_cols: int32 [48, 8], P('grp'), parts along dimension 0, may hold values from 0 to 23, as said below
- task_slot: int32 [48, 8], P('grp'), parts along dimension 0, may hold values from 0 to 7, each once within a row
Outputs:
- purified: float32 [48, 8, 128, 128], P(('grp', 'grid'), 'rep'), parts along dimension 0
There are 2 independent parts, one for each index of `grp`. A program takes and returns all parts, laid end to end along the dimension named above; each array names one. Nothing has to cross between parts.
Inputs may be any that keep to these rules, and one draw needn't show every extreme that they name: `block_cols`: the 8 block columns of a block row are distinct, the first is the row itself, and all lie among the block rows of the row's index of grid and of the two indices beside it, wrapping around: block row i of index g = i // 6 names columns ((6 * (g - 1) + c) mod 24) for c below 18.
All inputs are finite; a program needn't handle non-finite values.
Results may differ from a plain program's by a relative error of at most 0.00011.
Values sent between devices are 32-bit elements; how exact they have to be, the bound alone decides.
A program may use at most 64 MiB of HBM per device.

v0:
```python
import jax
import jax.numpy as jnp
from jax import lax
from jax.sharding import PartitionSpec as P


def shifted(shard, axis, by):
    devices = lax.axis_size(axis)
    return lax.ppermute(shard, axis, [(i, (i + by) % devices) for i in range(devices)])


def to_logical(blocks, task_slot, row_ids, slot_count):
    slot_ids = jnp.arange(slot_count, dtype=jnp.int32)
    permuted = task_slot[row_ids]
    inverse = jnp.sum(
        jnp.where(permuted[:, :, None] == slot_ids[None, None, :], slot_ids[None, :, None], 0),
        axis=1,
    )
    return jnp.take_along_axis(blocks, inverse[:, :, None, None], axis=1)


def local(task_blocks, block_cols, task_slot):
    row_count = task_blocks.shape[0]
    slots_here = task_blocks.shape[1]
    block_size = task_blocks.shape[2]
    block_total = block_cols.shape[0]
    slot_count = block_cols.shape[1]
    grid_place = lax.axis_index("grid")
    slice_rank = lax.axis_index("rep")
    first_row = row_count * (grid_place - 1)
    near_ids = (first_row + jnp.arange(3 * row_count, dtype=jnp.int32)) % block_total
    own_ids = row_count * grid_place + jnp.arange(row_count, dtype=jnp.int32)
    full_rows = lax.all_gather(task_blocks, "rep", axis=1, tiled=True)
    full_rows = to_logical(full_rows, task_slot, own_ids, slot_count)
    neighbours = []
    for offset in (1, -1):
        neighbours.append(shifted(full_rows, "grid", offset))
    near_rows = jnp.concatenate([neighbours[0], full_rows, neighbours[1]], axis=0)
    own_cols = block_cols[own_ids]
    near_cols = block_cols[near_ids]
    near_place = (own_cols - first_row) % block_total
    inner_cols = near_cols[near_place]
    matches = inner_cols[:, :, None, :] == own_cols[:, None, :, None]
    present = jnp.any(matches, axis=-1).astype(jnp.float32)
    chosen = jnp.argmax(matches.astype(jnp.int32), axis=-1)
    lookup = near_place[:, :, None] * slot_count + chosen
    flat_blocks = near_rows.reshape(3 * row_count * slot_count, block_size, block_size)

    def fetch(sub_lookup, sub_present):
        picked = jnp.take(flat_blocks, sub_lookup.reshape(-1), axis=0)
        picked = picked.reshape(sub_lookup.shape + (block_size, block_size))
        return picked * sub_present[:, :, :, None, None]

    slot_start = slice_rank * slots_here
    first_factor = fetch(
        lax.dynamic_slice_in_dim(lookup, slot_start, slots_here, 1),
        lax.dynamic_slice_in_dim(present, slot_start, slots_here, 1),
    )
    left_blocks = lax.dynamic_slice_in_dim(full_rows, slot_start, slots_here, 1)
    square_part = jnp.einsum(
        "ikab,ikmbc->imac", left_blocks, first_factor, precision=lax.Precision.HIGHEST
    )
    square_full = lax.psum(square_part, "rep")
    square_here = lax.dynamic_slice_in_dim(square_full, slot_start, slots_here, 1)
    second_factor = fetch(
        lax.dynamic_slice_in_dim(lookup, slot_start, slots_here, 2),
        lax.dynamic_slice_in_dim(present, slot_start, slots_here, 2),
    )
    cubed_here = jnp.einsum(
        "ikab,ikmbc->imac", square_full, second_factor, precision=lax.Precision.HIGHEST
    )
    return 3.0 * square_here - 2.0 * cubed_here


def solution(mesh):
    return jax.shard_map(
        local,
        mesh=mesh,
        in_specs=(P(("grp", "grid"), "rep", None, None), P("grp", None), P("grp", None)),
        out_specs=P(("grp", "grid"), "rep", None, None),
        check_vma=False,
    )
```

profile of v0, /device:TPU:0, one launch (start us, length us, event | category | flops | bytes accessed | tf_op | source)
XLA Modules:
  0.0 305.0 jit_solution(39726352822359116)
XLA Ops:
  6.5 0.7 all-gather.2.cloned.1.call-update
  7.3 0.8 copy.18
  8.1 0.6 gather_fusion
  8.8 31.3 %all-gather.2.cloned.1.call-done = f32[6,8,128,128]{3,2,1,0:T(8,128)} async-done(((f32[6,2,128,128]{3,2,1,0:T(8,128)}), f32[6,8,128,128]{3,2,1,0:T(8,128)}) %all-gather.2.cloned.1.call-update) | async-done | bytes 3145744 | tf_op jit(solution)/shard_map/all_gather | solution.py:33
  40.2 4.5 %gather_fusion.4 = f32[48,128,128]{2,1,0:T(8,128)} fusion(f32[6,8,128,128]{3,2,1,0:T(8,128)} %all-gather.2.cloned.1.call-done, s32[48]{0:T(128)S(1)} %reshape.196), kind=kCustom, calls=%fused_computation.6 | custom fusion | bytes 6291840 | tf_op jit(solution)/shard_map/jit(take_along_axis)/gather | solution.py:19
  44.6 2.2 broadcast_select_fusion.2
  46.8 1.5 collective-permute-start
  48.3 2.3 collective-permute-start.1
  50.8 0.6 gather_fusion.1
  51.4 0.6 gather_fusion.2
  52.0 0.6 gather_fusion.3
  52.6 2.4 fusion.32
  55.4 1.0 compare_reduce_fusion
  56.5 63.3 %collective-permute-done = f32[6,8,128,128]{3,2,1,0:T(8,128)} collective-permute-done((f32[6,8,128,128]{3,2,1,0:T(8,128)S(1)}, f32[6,8,128,128]{3,2,1,0:T(8,128)}, u32[]{:S(2)}, u32[]{:S(2)}) %collective-permute-start) | collective-permute-done | bytes 3145760 | tf_op jit(solution)/shard_map/ppermute | solution.py:9
  119.7 66.1 %collective-permute-done.1 = f32[6,8,128,128]{3,2,1,0:T(8,128)} collective-permute-done((f32[6,8,128,128]{3,2,1,0:T(8,128)S(1)}, f32[6,8,128,128]{3,2,1,0:T(8,128)}, u32[]{:S(2)}, u32[]{:S(2)}) %collective-permute-start.1) | collective-permute-done | bytes 3145760 | tf_op jit(solution)/shard_map/ppermute | solution.py:9
  185.8 7.6 %pad_maximum_fusion = f32[18,8,128,128]{3,2,1,0:T(8,128)} fusion(f32[6,8,128,128]{3,2,1,0:T(8,128)} %collective-permute-done.1, f32[6,8,128,128]{3,2,1,0:T(8,128)S(1)} %broadcast_select_fusion.2, f32[6,8,128,128]{3,2,1,0:T(8,128)} %collective-permute-done), kind=kLoop, calls=%fused_computation.7 | loop fusion | flops 4718592 | bytes 18874368 | tf_op jit(solution)/shard_map/concatenate | solution.py:38
  193.5 7.3 %gather_fusion.5 = f32[96,128,128]{2,1,0:T(8,128)} fusion(f32[144,128,128]{2,1,0:T(8,128)} %bitcast.69, s32[1024]{0:T(1024)S(1)} %pad_clamp_fusion.1), kind=kCustom, calls=%fused_computation.clone | custom fusion | bytes 12583296 | tf_op jit(solution)/shard_map/jit(_take)/gather | solution.py:50
  200.8 3.3 %broadcast_select_fusion.1 = f32[96,128,128]{2,1,0:T(8,128)S(1)} fusion(f32[96,128,128]{2,1,0:T(8,128)} %gather_fusion.5, pred[96]{0:T(512)(128)(4,1)S(1)} %get-tuple-element.11), kind=kLoop, calls=%fused_computation.14 | loop fusion | flops 1572864 | bytes 12583008 | tf_op jit(solution)/shard_map/jit(_take)/select_n | solution.py:50
  204.0 12.0 %fusion.7 = f32[6,8,128,128]{2,3,1,0:T(8,128)} fusion(f32[6,2,8,128,128]{4,3,2,1,0:T(8,128)S(1)} %bitcast.72, f32[6,2,8]{2,1,0:T(2,128)S(1)} %constant_dynamic-slice_fusion.2, f32[6,8,128,128]{3,2,1,0:T(8,128)S(1)} %broadcast_select_fusion.2, s32[]{:T(128)S(6)} %select_n.121), kind=kOutput, calls=%fused_computation.17 | convolution fusion | flops 2417491968 | bytes 10229764 | tf_op jit(solution)/shard_map/ikab,ikmbc->imac/dot_general | solution.py:60
  216.1 7.3 %gather_fusion.6 = f32[96,128,128]{2,1,0:T(8,128)} fusion(f32[144,128,128]{2,1,0:T(8,128)} %bitcast.70, s32[1024]{0:T(1024)S(1)} %pad_clamp_fusion), kind=kCustom, calls=%fused_computation.1.clone | custom fusion | bytes 12583296 | tf_op jit(solution)/shard_map/jit(_take)/gather | solution.py:50
  223.4 6.0 %broadcast_select_fusion = f32[96,128,128]{2,1,0:T(8,128)} fusion(f32[96,128,128]{2,1,0:T(8,128)} %gather_fusion.6, pred[96]{0:T(512)(128)(4,1)S(1)} %get-tuple-element.10), kind=kLoop, calls=%fused_computation.13 | loop fusion | flops 1572864 | bytes 12583008 | tf_op jit(solution)/shard_map/jit(_take)/select_n | solution.py:50
  229.4 54.0 %all-reduce.2.cloned.1.call-done = f32[6,8,128,128]{2,3,1,0:T(8,128)} async-done(((f32[6,8,128,128]{2,3,1,0:T(8,128)}), f32[6,8,128,128]{2,3,1,0:T(8,128)}) %all-reduce.2.cloned.1.call-update) | async-done | bytes 3145744 | tf_op jit(solution)/shard_map/psum | solution.py:63
  283.4 13.6 %fusion.25 = f32[6,2,128,128]{2,3,1,0:T(8,128)S(1)} fusion(f32[6,8,128,128]{2,3,1,0:T(8,128)} %all-reduce.2.cloned.1.call-done, f32[6,8,2,128,128]{4,3,2,1,0:T(8,128)} %bitcast.71, f32[6,8,2]{2,1,0:T(8,128)S(1)} %constant_dynamic-slice_fusion, s32[]{:T(128)S(6)} %select_n.121), kind=kOutput, calls=%fused_computation.22 | convolution fusion | flops 2418081792 | bytes 11010436 | tf_op jit(solution)/shard_map/ikab,ikmbc->imac/dot_general | solution.py:69
  297.0 1.1 copy.22
  (30 shorter events, 1.0 us)
Async XLA Ops:
  6.5 33.6 %all-gather.2.cloned.1.call-start = ((), (), s32[]{:S(2)}) async-start(), calls=%async_computation | async-start | bytes 3932160 | tf_op jit(solution)/shard_map/all_gather | solution.py:33
  7.3 276.2 %all-reduce.2.cloned.1.call-start = ((), (), s32[]{:S(2)}) async-start(), calls=%async_computation.1 | async-start | bytes 6291456 | tf_op jit(solution)/shard_map/psum | solution.py:63
  8.8 41.9 %copy-start = (s32[24,8]{0,1:T(8,128)S(1)}, s32[24,8]{0,1:T(8,128)}, u32[]{:S(2)}) copy-start(s32[24,8]{0,1:T(8,128)} %param.6) | copy-start | bytes 2308
  46.8 72.9 %collective-permute-start = (f32[6,8,128,128]{3,2,1,0:T(8,128)S(1)}, f32[6,8,128,128]{3,2,1,0:T(8,128)}, u32[]{:S(2)}, u32[]{:S(2)}) collective-permute-start(f32[6,8,128,128]{3,2,1,0:T(8,128)S(1)} %broadcast_select_fusion.2), channel_id=1, source_target_pairs={{0,4},{4,8},{8,12},{12,0},{1,5},{5,9},{9,13},{13,1},{2,6},{6,10},{... | collective-permute-start | bytes 9437192 | tf_op jit(solution)/shard_map/ppermute | solution.py:9
  48.3 137.5 %collective-permute-start.1 = (f32[6,8,128,128]{3,2,1,0:T(8,128)S(1)}, f32[6,8,128,128]{3,2,1,0:T(8,128)}, u32[]{:S(2)}, u32[]{:S(2)}) collective-permute-start(f32[6,8,128,128]{3,2,1,0:T(8,128)S(1)} %broadcast_select_fusion.2), channel_id=1, source_target_pairs={{0,12},{4,0},{8,4},{12,8},{1,13},{5,1},{9,5},{13,9},{2,14},{6,2},{... | collective-permute-start | bytes 9437192 | tf_op jit(solution)/shard_map/ppermute | solution.py:9
Sparse Core Ops, SparseCore 0:
  8.9 31.2 all-gather.1
  216.2 67.2 all-reduce.1
where the time goes:
time: 305 us
  waiting for transfers between devices  215 us (70%)
  matrix products  25.5 us (8%)
  local copies, waits for them, and re-layouts  23.9 us (8%)
  other arithmetic  22.7 us (7%)
  between operations  13.6 us (4%)
  starting transfers between devices  3.92 us (1%)
    ppermute x2, waiting for transfers between devices, shifted(): lax.ppermute(shard, axis, [(i, (i + by) % devices) for i in range(devices)])  129 us
    psum x1, waiting for transfers between devices, local(): square_full = lax.psum(square_part, 'rep')  54 us
    all_gather x1, waiting for transfers between devices, local(): full_rows = lax.all_gather(task_blocks, 'rep', axis=1, tiled=True)  31.3 us
    gather x2, local copies, waits for them, and re-layouts, fetch(): picked = jnp.take(flat_blocks, sub_lookup.reshape(-1), axis=0)  14.6 us
    dot_general x1, matrix products, local(): jnp.einsum('ikab,ikmbc->imac', square_full, second_factor, precision=lax....  13.6 us
    dot_general x1, matrix products, local(): jnp.einsum('ikab,ikmbc->imac', left_blocks, first_factor, precision=lax.P...  12 us
    select_n x3, other arithmetic, fetch(): picked = jnp.take(flat_blocks, sub_lookup.reshape(-1), axis=0)  9.24 us
    concatenate x1, other arithmetic, local(): jnp.concatenate([neighbours[0], full_rows, neighbours[1]], axis=0)  7.63 us
  transfers between devices with their start and end apart: 4, of which 4 were waited for; matrix products, arithmetic and copies ran while one was open for 7% of the time, Pallas kernels for 0%

commit v1 on v0

v1 whole, which is shorter than its diff:
```python
import functools

import jax
import jax.numpy as jnp
from jax import lax
from jax.experimental import pallas as pl
from jax.experimental.pallas import tpu as pltpu
from jax.sharding import PartitionSpec as P

MESH = pl.DeviceIdType.MESH


def lookup_tables(block_cols, task_slot, row_count):
    block_total, slot_count = block_cols.shape
    grid_place = lax.axis_index("grid")
    first_row = row_count * (grid_place - 1)
    near_count = 3 * row_count
    near_ids = (first_row + jnp.arange(near_count, dtype=jnp.int32)) % block_total
    near_cols = block_cols[near_ids]
    near_slot = task_slot[near_ids]
    slots = jnp.arange(slot_count, dtype=jnp.int32)
    hot = near_slot[:, :, None] == slots[None, None, :]
    near_task = jnp.sum(jnp.where(hot, near_cols[:, None, :], 0), axis=2)
    own_cols = near_cols[row_count : 2 * row_count]
    own_task = near_task[row_count : 2 * row_count]
    places = jnp.arange(near_count, dtype=jnp.int32)
    tile = (
        (places // row_count)[:, None] * (slot_count // 2) + slots[None, :] // 2
    ) * row_count + (places % row_count)[:, None]
    code = 4 * tile + slots[None, :] % 2
    match = near_task[None, :, None, :] == own_cols[:, None, :, None]
    found = 2 + jnp.sum(jnp.where(match, code[None, :, None, :] - 2, 0), axis=3)
    left_cols = jnp.stack([own_task, own_cols])
    left_place = (left_cols - first_row) % block_total
    pick = left_place[:, :, :, None] == places
    table = jnp.sum(jnp.where(pick[..., None], found[None, :, None], 0), axis=3)
    return table.reshape(2, -1)


def kernel(
    grid_size, table, task_ref, out_ref,
    own, stage, left, near, near_hi, near_lo, square, out_stage, landed,
    task_sem, z_send, z_recv, x_send, x_recv, s_send, s_recv,
    l_send, l_recv, q_send, q_recv, o_send, o_recv,
):
    row_count, _, size, _ = own.shape
    half = size // 2
    slot_count = 2 * left.shape[0]
    grid_place = lax.axis_index("grid")
    rep = lax.axis_index("rep")
    side = rep // 2
    part = rep % 2
    sib = 2 * side + 1 - part
    ctr = 2 * (1 - side) + part
    diag = 2 * (1 - side) + 1 - part
    up = lax.rem(grid_place + 1, grid_size)
    down = lax.rem(grid_place + grid_size - 1, grid_size)

    def remote(src, dst, send, recv, **where):
        return pltpu.make_async_remote_copy(
            src_ref=src, dst_ref=dst, send_sem=send, recv_sem=recv,
            device_id=where, device_id_type=MESH,
        )

    fetch = pltpu.make_async_copy(task_ref, own, task_sem)
    fetch.start()
    barrier = pltpu.get_barrier_semaphore()
    for where in ({"grid": up}, {"grid": down}, {"rep": sib}, {"rep": ctr}, {"rep": diag}):
        pl.semaphore_signal(barrier, inc=1, device_id=where, device_id_type=MESH)
    fetch.wait()

    low_lanes = lax.broadcasted_iota(jnp.int32, (size, size), 1) < half

    def swap(first, second):
        low = low_lanes[: first.shape[0]]
        return (
            jnp.where(low, first, pltpu.roll(second, half, 1)),
            jnp.where(low, pltpu.roll(first, half, 1), second),
        )

    @pl.loop(0, row_count)
    def _(i):
        packed = swap(own[i, 0], own[i, 1])
        near[1, rep, i] = jnp.where(side == 0, packed[0], packed[1])
        stage[i] = jnp.where(side == 0, packed[1], packed[0])

    pl.semaphore_wait(barrier, 5)

    to_ctr = remote(stage, near.at[1, rep], x_send, x_recv, rep=ctr)
    to_ctr.start()

    def z_copy(n, source):
        return remote(
            near.at[1, source], near.at[2 * (n % 2), source],
            z_send.at[n], z_recv.at[n], grid=up if n % 2 == 0 else down,
        )

    z_own = [z_copy(n, rep) for n in (0, 1)]
    for copy in z_own:
        copy.start()

    def s_copy(n, direction, source):
        return remote(
            near.at[direction, source], near.at[direction, source],
            s_send.at[n], s_recv.at[n], rep=sib,
        )

    s_copies = [
        s_copy(0, 1, rep), s_copy(1, 1, ctr), s_copy(2, 0, rep),
        s_copy(3, 2, rep), s_copy(4, 0, ctr), s_copy(5, 2, ctr),
    ]
    s_copies[0].start()

    def left_rows(which):
        return own.at[:, :, pl.ds(pl.multiple_of(which * half, half), half), :]

    lefts = [
        remote(left_rows(1 - part), left.at[rep], l_send.at[0], l_recv.at[0], rep=sib),
        remote(left_rows(part), left.at[rep], l_send.at[1], l_recv.at[1], rep=ctr),
        remote(left_rows(1 - part), left.at[rep], l_send.at[2], l_recv.at[2], rep=diag),
    ]
    lefts[0].start()

    @pl.loop(0, row_count)
    def _(i):
        for n in range(2):
            left[rep, i, n] = own[i, n, pl.ds(pl.multiple_of(part * half, half), half), :]

    def split(value):
        high = value.astype(jnp.bfloat16)
        return high, (value - high.astype(jnp.float32)).astype(jnp.bfloat16)

    def convert(direction, source):
        base = (direction * (slot_count // 2) + source) * row_count

        @pl.loop(0, row_count)
        def _(i):
            high, low = split(near[direction, source, i])
            near_hi[base + i] = high
            near_lo[base + i] = low

    convert(1, rep)
    to_ctr.wait_recv()
    z_ctr = [z_copy(n, ctr) for n in (2, 3)]
    for copy in z_ctr:
        copy.start()
    s_copies[1].start()
    to_ctr.wait_send()
    lefts[1].start()
    lefts[2].start()
    convert(1, ctr)
    s_copies[0].wait_recv()
    convert(1, sib)
    s_copies[1].wait_recv()
    convert(1, diag)
    for copy, onward, direction in zip(z_own, s_copies[2:4], (0, 2)):
        copy.wait_recv()
        onward.start()
        convert(direction, rep)
    for onward, direction in zip(s_copies[2:4], (0, 2)):
        onward.wait_recv()
        convert(direction, sib)
    for copy in lefts:
        copy.wait_recv()
    for copy, onward, direction in zip(z_ctr, s_copies[4:6], (0, 2)):
        copy.wait_recv()
        onward.start()
        convert(direction, ctr)
    for onward, direction in zip(s_copies[4:6], (0, 2)):
        onward.wait_recv()
        convert(direction, diag)

    lane_half = lax.broadcasted_iota(jnp.int32, (size, size), 1) // half
    nothing = jnp.zeros((size, size), jnp.bfloat16)

    def products(which, i, pair, lhs):
        total = jnp.zeros((half, 2 * size), jnp.float32)
        for s in range(0, slot_count, 2):
            highs, lows = [], []
            for t in (s, s + 1):
                high_row, low_row = [], []
                for m in range(2):
                    code = table[which, (i * slot_count + t) * slot_count + 2 * pair + m]
                    tile = code // 4
                    keep = lane_half == code % 4
                    high_row.append(jnp.where(keep, near_hi[tile], nothing))
                    low_row.append(jnp.where(keep, near_lo[tile], nothing))
                highs.append(jnp.concatenate(high_row, axis=1))
                lows.append(jnp.concatenate(low_row, axis=1))
            both = lhs[:, s * size : (s + 2) * size]
            wide = jnp.dot(
                both, jnp.concatenate(highs, axis=0), preferred_element_type=jnp.float32
            )
            total += wide[:half] + wide[half:] + jnp.dot(
                both[:half], jnp.concatenate(lows, axis=0), preferred_element_type=jnp.float32
            )
        first, second = total[:, :size], total[:, size:]
        return jnp.where(
            low_lanes[:half], first + pltpu.roll(first, half, 1), second + pltpu.roll(second, half, 1)
        )

    def left_operand(tiles):
        high, low = split(jnp.concatenate(tiles, axis=1))
        return jnp.concatenate([high, low], axis=0)

    def square_copy(i):
        return remote(
            square.at[side, i], square.at[side, i], q_send.at[i], q_recv.at[i], rep=ctr
        )

    @pl.loop(0, row_count)
    def _(i):
        lhs = left_operand([left[t // 2, i, t % 2] for t in range(slot_count)])
        for pair in range(slot_count // 2):
            square[side, i, pair] = products(0, i, pair, lhs)
        square_copy(i).start()

    def out_copy(i, n, peer):
        return remote(
            out_stage.at[i, peer],
            landed.at[side, i, pl.ds(pl.multiple_of(part * half, half), half), :],
            o_send.at[n, i], o_recv.at[n, i], rep=peer,
        )

    peers = (diag, ctr, sib)

    @pl.loop(0, row_count)
    def _(i):
        square_copy(i).wait_recv()
        tiles = []
        for pair in range(slot_count // 2):
            tiles.extend(swap(square[0, i, pair], square[1, i, pair]))
        lhs = left_operand(tiles)
        for pair in range(slot_count // 2):
            cubed = products(1, i, pair, lhs)
            out_stage[i, pair] = 3.0 * square[side, i, pair] - 2.0 * cubed
        for n, peer in enumerate(peers):
            out_copy(i, n, peer).start()
        landed[side, i, pl.ds(pl.multiple_of(part * half, half), half), :] = out_stage[i, rep]

    @pl.loop(0, row_count)
    def _(i):
        for n, peer in enumerate(peers):
            out_copy(i, n, peer).wait_recv()
        first, second = swap(landed[0, i], landed[1, i])
        out_ref[i, 0] = first
        out_ref[i, 1] = second

    for copy in z_own + z_ctr + s_copies + lefts:
        copy.wait_send()

    @pl.loop(0, row_count)
    def _(i):
        square_copy(i).wait_send()
        for n, peer in enumerate(peers):
            out_copy(i, n, peer).wait_send()


def local(grid_size, rep_size, task_blocks, block_cols, task_slot):
    row_count, slots_here, size, _ = task_blocks.shape
    pairs = rep_size
    table = lookup_tables(block_cols, task_slot, row_count)
    half = size // 2
    f32, bf16 = jnp.float32, jnp.bfloat16
    dma = pltpu.SemaphoreType.DMA
    return pl.pallas_call(
        functools.partial(kernel, grid_size),
        out_shape=jax.ShapeDtypeStruct(task_blocks.shape, f32),
        in_specs=[
            pl.BlockSpec(memory_space=pltpu.SMEM),
            pl.BlockSpec(memory_space=pl.ANY),
        ],
        out_specs=pl.BlockSpec(memory_space=pltpu.VMEM),
        scratch_shapes=[
            pltpu.VMEM((row_count, slots_here, size, size), f32),
            pltpu.VMEM((row_count, size, size), f32),
            pltpu.VMEM((rep_size, row_count, slots_here, half, size), f32),
            pltpu.VMEM((3, rep_size, row_count, size, size), f32),
            pltpu.VMEM((3 * rep_size * row_count, size, size), bf16),
            pltpu.VMEM((3 * rep_size * row_count, size, size), bf16),
            pltpu.VMEM((2, row_count, pairs, half, size), f32),
            pltpu.VMEM((row_count, pairs, half, size), f32),
            pltpu.VMEM((2, row_count, size, size), f32),
            dma, dma((4,)), dma((4,)), dma, dma, dma((6,)), dma((6,)),
            dma((3,)), dma((3,)), dma((row_count,)), dma((row_count,)),
            dma((3, row_count)), dma((3, row_count)),
        ],
        compiler_params=pltpu.CompilerParams(
            collective_id=0, has_side_effects=True, vmem_limit_bytes=40 * 1024 * 1024
        ),
    )(table, task_blocks)


def solution(mesh):
    return jax.shard_map(
        functools.partial(local, mesh.shape["grid"], mesh.shape["rep"]),
        mesh=mesh,
        in_specs=(P(("grp", "grid"), "rep", None, None), P("grp", None), P("grp", None)),
        out_specs=P(("grp", "grid"), "rep", None, None),
        check_vma=False,
    )
```

time: 305 us -> 76.9 us (0.25)
  waiting for transfers between devices: 215 us -> 0 us
  Pallas kernels: 0 us -> 69.6 us
  matrix products: 25.5 us -> 0 us
  other arithmetic: 22.7 us -> 2.07 us
  local copies, waits for them, and re-layouts: 23.9 us -> 4.97 us
  between operations: 13.6 us -> 0.08 us
  starting transfers between devices: 3.92 us -> 0 us
    ppermute x2 -> x0, waiting for transfers between devices: 129 us -> none  [shifted(): lax.ppermute(shard, axis, [(i, (i + by) % devices) for i in range(devices)])]
    pallas_call x0 -> x1, Pallas kernels: none -> 69.6 us  [local(): pl.pallas_call(functools.partial(kernel, grid_size), out_shape=jax.ShapeD...]
    psum x1 -> x0, waiting for transfers between devices: 54 us -> none  [local(): square_full = lax.psum(square_part, 'rep')]
    all_gather x1 -> x0, waiting for transfers between devices: 31.3 us -> none  [local(): full_rows = lax.all_gather(task_blocks, 'rep', axis=1, tiled=True)]
    dot_general x2 -> x0, matrix products: 25.5 us -> none  [the longest x1 13.6 us: local(): jnp.einsum('ikab,ikmbc->imac', square_full, second_factor, precision=lax....]
    gather x8 -> x4, local copies, waits for them, and re-layouts: 21.4 us -> 1.28 us  [the longest x2 0.64 us: lookup_tables(): near_cols = block_cols[near_ids]]
    select_n x7 -> x4, other arithmetic: 11.4 us -> 0.05 us  [the longest x1 0.02 us: lookup_tables(): left_place = (left_cols - first_row) % block_total]
    concatenate x1 -> x0, other arithmetic: 7.63 us -> none  [local(): jnp.concatenate([neighbours[0], full_rows, neighbours[1]], axis=0)]
  transfers between devices with their start and end apart: 4 -> 0, of which waited for: 4 -> 0; matrix products, arithmetic and copies ran while one was open for 7% -> 0% of each run, Pallas kernels for 0% -> 0%
where the time goes in v1:
time: 76.9 us; the launch traced here: 76.7 us
  Pallas kernels  69.6 us (91%)
  local copies, waits for them, and re-layouts  4.97 us (6%)
  other arithmetic  2.07 us (3%)
    pallas_call x1, Pallas kernels, local(): pl.pallas_call(functools.partial(kernel, grid_size), out_shape=jax.ShapeD...  69.6 us
    unnamed x9, local copies, waits for them, and re-layouts  3.44 us
    reduce_sum x1, other arithmetic, lookup_tables(): table = jnp.sum(jnp.where(pick[..., None], found[None, :, None], 0), axis=3)  1.7 us

profile of v1, /device:TPU:0, one launch (start us, length us, event | category | flops | bytes accessed | tf_op | source)
XLA Modules:
  0.0 76.7 jit_solution(283386394340687671)
XLA Ops:
  0.0 0.0 copy-start.1
  0.1 0.1 add_add_fusion
  0.1 0.6 copy-done.1
  0.7 0.1 copy.8
  0.8 0.6 gather_fusion.1
  1.4 0.1 copy.9
  1.4 0.0 copy-start.2
  1.5 0.7 copy-done.2
  2.1 0.1 copy.6
  2.2 0.6 gather_fusion
  2.8 0.1 copy.7
  2.9 0.1 slice.6
  2.9 0.1 copy.10
  3.0 0.1 iota_compare_fusion
  3.1 0.1 select_reduce_fusion.1
  3.3 1.7 %select_reduce_fusion = s32[2,6,8,8]{3,2,1,0:T(8,128)S(1)} fusion(s32[6,18,8]{1,2,0:T(8,128)S(1)} %broadcast_add_fusion, pred[2,6,8,18]{3,2,1,0:T(8,128)(4,1)S(1)} %iota_compare_fusion), kind=kLoop, calls=%fused_computation.2 | loop fusion | flops 26880 | bytes 8256 | tf_op jit(solution)/shard_map/reduce_sum | solution.py:36
  5.0 0.1 reshape.200.table
  5.1 0.0 copy-start
  5.1 1.1 %copy-done = f32[6,2,128,128]{3,2,1,0:T(8,128)S(1)} copy-done((f32[6,2,128,128]{3,2,1,0:T(8,128)S(1)}, f32[6,2,128,128]{3,2,1,0:T(8,128)}, u32[]{:S(2)}) %copy-start) | copy-done | bytes 786456
  6.2 69.6 %shard_map.37 = f32[6,2,128,128]{3,2,1,0:T(8,128)S(1)} custom-call(s32[2,384]{1,0:T(2,128)S(1)} %reshape.200.table, f32[6,2,128,128]{3,2,1,0:T(8,128)S(1)} %copy-done), custom_call_target="tpu_custom_call" | custom-call | tf_op jit(solution)/shard_map/pallas_call | solution.py:266
  75.8 0.9 %copy.12 = f32[6,2,128,128]{3,2,1,0:T(8,128)} copy(f32[6,2,128,128]{3,2,1,0:T(8,128)S(1)} %shard_map.37) | data formatting | bytes 1572864
  (8 shorter events, 0.1 us)
Async XLA Ops:
  0.0 0.7 copy-start.1
  1.4 0.7 copy-start.2
  5.1 1.1 %copy-start = (f32[6,2,128,128]{3,2,1,0:T(8,128)S(1)}, f32[6,2,128,128]{3,2,1,0:T(8,128)}, u32[]{:S(2)}) copy-start(f32[6,2,128,128]{3,2,1,0:T(8,128)} %task_ref.1) | copy-start | bytes 2359300

commit v2 on v1

--- a/solution.py
+++ b/solution.py
@@ -10,37 +10,11 @@
 MESH = pl.DeviceIdType.MESH
 
 
-def lookup_tables(block_cols, task_slot, row_count):
-    block_total, slot_count = block_cols.shape
-    grid_place = lax.axis_index("grid")
-    first_row = row_count * (grid_place - 1)
-    near_count = 3 * row_count
-    near_ids = (first_row + jnp.arange(near_count, dtype=jnp.int32)) % block_total
-    near_cols = block_cols[near_ids]
-    near_slot = task_slot[near_ids]
-    slots = jnp.arange(slot_count, dtype=jnp.int32)
-    hot = near_slot[:, :, None] == slots[None, None, :]
-    near_task = jnp.sum(jnp.where(hot, near_cols[:, None, :], 0), axis=2)
-    own_cols = near_cols[row_count : 2 * row_count]
-    own_task = near_task[row_count : 2 * row_count]
-    places = jnp.arange(near_count, dtype=jnp.int32)
-    tile = (
-        (places // row_count)[:, None] * (slot_count // 2) + slots[None, :] // 2
-    ) * row_count + (places % row_count)[:, None]
-    code = 4 * tile + slots[None, :] % 2
-    match = near_task[None, :, None, :] == own_cols[:, None, :, None]
-    found = 2 + jnp.sum(jnp.where(match, code[None, :, None, :] - 2, 0), axis=3)
-    left_cols = jnp.stack([own_task, own_cols])
-    left_place = (left_cols - first_row) % block_total
-    pick = left_place[:, :, :, None] == places
-    table = jnp.sum(jnp.where(pick[..., None], found[None, :, None], 0), axis=3)
-    return table.reshape(2, -1)
-
-
 def kernel(
-    grid_size, table, task_ref, out_ref,
+    grid_size, task_ref, cols_ref, slots_ref, out_ref,
+    cols, slots, cols_smem, slots_smem, near_cols, near_slots, codes_vmem, codes,
     own, stage, left, near, near_hi, near_lo, square, out_stage, landed,
-    task_sem, z_send, z_recv, x_send, x_recv, s_send, s_recv,
+    task_sem, meta_sem, z_send, z_recv, x_send, x_recv, s_send, s_recv,
     l_send, l_recv, q_send, q_recv, o_send, o_recv,
 ):
     row_count, _, size, _ = own.shape
@@ -64,6 +38,14 @@
 
     fetch = pltpu.make_async_copy(task_ref, own, task_sem)
     fetch.start()
+    meta = [
+        pltpu.make_async_copy(src, dst, meta_sem.at[n])
+        for n, (src, dst) in enumerate((
+            (cols_ref, cols), (slots_ref, slots), (cols_ref, cols_smem), (slots_ref, slots_smem)
+        ))
+    ]
+    for copy in meta:
+        copy.start()
     barrier = pltpu.get_barrier_semaphore()
     for where in ({"grid": up}, {"grid": down}, {"rep": sib}, {"rep": ctr}, {"rep": diag}):
         pl.semaphore_signal(barrier, inc=1, device_id=where, device_id_type=MESH)
@@ -139,7 +121,34 @@
             near_hi[base + i] = high
             near_lo[base + i] = low
 
+    for copy in meta:
+        copy.wait()
+    pad = near_cols.shape[0] // 3
+    for d in range(3):
+        start = row_count * lax.rem(grid_place + grid_size + d - 1, grid_size)
+        for i in range(row_count):
+            near_cols[pl.ds(d * pad + i, 1), :] = cols[pl.ds(start + i, 1), :]
+            near_slots[pl.ds(d * pad + i, 1), :] = slots[pl.ds(start + i, 1), :]
+    rows = lax.broadcasted_iota(jnp.int32, near_cols.shape, 0)
+    slot_ids = lax.broadcasted_iota(jnp.int32, near_cols.shape, 1)
+    by_col, by_task = near_cols[...], near_slots[...]
+    tile = (rows // pad) * (slot_count // 2) * row_count + rows % pad
+    last_code = 4 * near_hi.shape[0] - 1
+    coded = jnp.zeros(near_cols.shape, jnp.int32)
+    for t in range(slot_count):
+        coded += jnp.where(
+            by_task[:, t : t + 1] == slot_ids, 4 * (tile + (t // 2) * row_count) + t % 2 - 2, 0
+        )
+    for i in range(row_count):
+        mine = near_cols[pl.ds(pad + i, 1), :]
+        found = jnp.full(near_cols.shape, 2, jnp.int32)
+        for n in range(slot_count):
+            found += jnp.where(by_col[:, n : n + 1] == mine, coded[:, n : n + 1], 0)
+        codes_vmem[:, i * slot_count : (i + 1) * slot_count] = jnp.clip(found, 0, last_code)
+    to_smem = pltpu.make_async_copy(codes_vmem, codes, meta_sem.at[4])
+    to_smem.start()
     convert(1, rep)
+    to_smem.wait()
     to_ctr.wait_recv()
     z_ctr = [z_copy(n, ctr) for n in (2, 3)]
     for copy in z_ctr:
@@ -173,14 +182,26 @@
     lane_half = lax.broadcasted_iota(jnp.int32, (size, size), 1) // half
     nothing = jnp.zeros((size, size), jnp.bfloat16)
 
-    def products(which, i, pair, lhs):
+    first_row = row_count * (grid_place - 1)
+    block_total = row_count * grid_size
+
+    def near_place(i, s, in_task_order):
+        row = row_count * grid_place + i
+        slot = slots_smem[row, s] if in_task_order else s
+        place = cols_smem[row, slot] - first_row
+        place = jnp.where(place < 0, place + block_total, place)
+        place = jnp.where(place >= block_total, place - block_total, place)
+        place = jnp.clip(place, 0, 3 * row_count - 1)
+        return place + (pad - row_count) * (place // row_count)
+
+    def products(places, i, pair, lhs):
         total = jnp.zeros((half, 2 * size), jnp.float32)
         for s in range(0, slot_count, 2):
             highs, lows = [], []
             for t in (s, s + 1):
                 high_row, low_row = [], []
                 for m in range(2):
-                    code = table[which, (i * slot_count + t) * slot_count + 2 * pair + m]
+                    code = codes[places[t], i * slot_count + 2 * pair + m]
                     tile = code // 4
                     keep = lane_half == code % 4
                     high_row.append(jnp.where(keep, near_hi[tile], nothing))
@@ -210,9 +231,10 @@
 
     @pl.loop(0, row_count)
     def _(i):
+        places = [near_place(i, s, True) for s in range(slot_count)]
         lhs = left_operand([left[t // 2, i, t % 2] for t in range(slot_count)])
         for pair in range(slot_count // 2):
-            square[side, i, pair] = products(0, i, pair, lhs)
+            square[side, i, pair] = products(places, i, pair, lhs)
         square_copy(i).start()
 
     def out_copy(i, n, peer):
@@ -227,12 +249,13 @@
     @pl.loop(0, row_count)
     def _(i):
         square_copy(i).wait_recv()
+        places = [near_place(i, s, False) for s in range(slot_count)]
         tiles = []
         for pair in range(slot_count // 2):
             tiles.extend(swap(square[0, i, pair], square[1, i, pair]))
         lhs = left_operand(tiles)
         for pair in range(slot_count // 2):
-            cubed = products(1, i, pair, lhs)
+            cubed = products(places, i, pair, lhs)
             out_stage[i, pair] = 3.0 * square[side, i, pair] - 2.0 * cubed
         for n, peer in enumerate(peers):
             out_copy(i, n, peer).start()
@@ -259,7 +282,9 @@
 def local(grid_size, rep_size, task_blocks, block_cols, task_slot):
     row_count, slots_here, size, _ = task_blocks.shape
     pairs = rep_size
-    table = lookup_tables(block_cols, task_slot, row_count)
+    pad = -(-row_count // 8) * 8
+    slot_count = block_cols.shape[1]
+    i32 = jnp.int32
     half = size // 2
     f32, bf16 = jnp.float32, jnp.bfloat16
     dma = pltpu.SemaphoreType.DMA
@@ -267,11 +292,20 @@
         functools.partial(kernel, grid_size),
         out_shape=jax.ShapeDtypeStruct(task_blocks.shape, f32),
         in_specs=[
-            pl.BlockSpec(memory_space=pltpu.SMEM),
-            pl.BlockSpec(memory_space=pl.ANY),
+            pl.BlockSpec(memory_space=pltpu.HBM),
+            pl.BlockSpec(memory_space=pltpu.HBM),
+            pl.BlockSpec(memory_space=pltpu.HBM),
         ],
         out_specs=pl.BlockSpec(memory_space=pltpu.VMEM),
         scratch_shapes=[
+            pltpu.VMEM(block_cols.shape, i32),
+            pltpu.VMEM(block_cols.shape, i32),
+            pltpu.SMEM(block_cols.shape, i32),
+            pltpu.SMEM(block_cols.shape, i32),
+            pltpu.VMEM((3 * pad, slot_count), i32),
+            pltpu.VMEM((3 * pad, slot_count), i32),
+            pltpu.VMEM((3 * pad, 128), i32),
+            pltpu.SMEM((3 * pad, 128), i32),
             pltpu.VMEM((row_count, slots_here, size, size), f32),
             pltpu.VMEM((row_count, size, size), f32),
             pltpu.VMEM((rep_size, row_count, slots_here, half, size), f32),
@@ -281,14 +315,14 @@
             pltpu.VMEM((2, row_count, pairs, half, size), f32),
             pltpu.VMEM((row_count, pairs, half, size), f32),
             pltpu.VMEM((2, row_count, size, size), f32),
-            dma, dma((4,)), dma((4,)), dma, dma, dma((6,)), dma((6,)),
+            dma, dma((5,)), dma((4,)), dma((4,)), dma, dma, dma((6,)), dma((6,)),
             dma((3,)), dma((3,)), dma((row_count,)), dma((row_count,)),
             dma((3, row_count)), dma((3, row_count)),
         ],
         compiler_params=pltpu.CompilerParams(
-            collective_id=0, has_side_effects=True, vmem_limit_bytes=40 * 1024 * 1024
+            collective_id=0, has_side_effects=True, vmem_limit_bytes=62 * 1024 * 1024
         ),
-    )(table, task_blocks)
+    )(task_blocks, block_cols, task_slot)
 
 
 def solution(mesh):

time: 76.9 us -> 75.1 us (0.977)
  other arithmetic: 2.07 us -> 0 us
  Pallas kernels: 69.6 us -> 70.8 us
  local copies, waits for them, and re-layouts: 4.97 us -> 4.1 us
    reduce_sum x3 -> x0, other arithmetic: 1.85 us -> none  [the longest x1 1.7 us: lookup_tables(): table = jnp.sum(jnp.where(pick[..., None], found[None, :, None], 0), axis=3)]
    gather x4 -> x0, local copies, waits for them, and re-layouts: 1.28 us -> none  [the longest x2 0.64 us: lookup_tables(): near_cols = block_cols[near_ids]]
    pallas_call x1, Pallas kernels: 69.6 us -> 70.8 us  [local(): pl.pallas_call(functools.partial(kernel, grid_size), out_shape=jax.ShapeD...]
    unnamed x9 -> x5, local copies, waits for them, and re-layouts: 3.44 us -> 4.1 us
where the time goes in v2:
time: 75.1 us; the launch traced here: 74.9 us
  Pallas kernels  70.8 us (94%)
  local copies, waits for them, and re-layouts  4.1 us (5%)
    pallas_call x1, Pallas kernels, local(): pl.pallas_call(functools.partial(kernel, grid_size), out_shape=jax.ShapeD...  70.8 us
    unnamed x5, local copies, waits for them, and re-layouts  4.1 us

profile of v2, /device:TPU:0, one launch (start us, length us, event | category | flops | bytes accessed | tf_op | source)
XLA Modules:
  0.0 74.9 jit_solution(6442841901647735288)
XLA Ops:
  0.0 0.0 copy-start
  0.0 1.4 %copy.4.cols_ref = s32[24,8]{1,0:T(8,128)} copy(s32[24,8]{0,1:T(8,128)} %param.4) | data formatting | bytes 1536 | tf_op args[1]
  1.4 0.0 copy-done
  1.4 0.7 copy.5.slots_ref
  2.0 70.8 %shard_map.37 = f32[6,2,128,128]{3,2,1,0:T(8,128)} custom-call(f32[6,2,128,128]{3,2,1,0:T(8,128)} %task_ref.1, s32[24,8]{1,0:T(8,128)} %copy.4.cols_ref, s32[24,8]{1,0:T(8,128)} %copy.5.slots_ref), custom_call_target="tpu_custom_call" | custom-call | tf_op jit(solution)/shard_map/pallas_call | solution.py:291
  72.8 2.1 %copy.7 = f32[6,2,128,128]{3,2,1,0:T(8,128)} copy(f32[6,2,128,128]{3,2,1,0:T(8,128)} %shard_map.37) | data formatting | bytes 1572864
Async XLA Ops:
  0.0 1.4 %copy-start = (s32[24,8]{0,1:T(8,128)S(1)}, s32[24,8]{0,1:T(8,128)}, u32[]{:S(2)}) copy-start(s32[24,8]{0,1:T(8,128)} %param.5) | copy-start | bytes 2308

commit v3 on v2

--- a/solution.py
+++ b/solution.py
@@ -12,7 +12,7 @@
 
 def kernel(
     grid_size, task_ref, cols_ref, slots_ref, out_ref,
-    cols, slots, cols_smem, slots_smem, near_cols, near_slots, codes_vmem, codes,
+    cols, slots, cols_smem, slots_smem, codes_vmem, codes,
     own, stage, left, near, near_hi, near_lo, square, out_stage, landed,
     task_sem, meta_sem, z_send, z_recv, x_send, x_recv, s_send, s_recv,
     l_send, l_recv, q_send, q_recv, o_send, o_recv,
@@ -123,28 +123,30 @@
 
     for copy in meta:
         copy.wait()
-    pad = near_cols.shape[0] // 3
-    for d in range(3):
-        start = row_count * lax.rem(grid_place + grid_size + d - 1, grid_size)
-        for i in range(row_count):
-            near_cols[pl.ds(d * pad + i, 1), :] = cols[pl.ds(start + i, 1), :]
-            near_slots[pl.ds(d * pad + i, 1), :] = slots[pl.ds(start + i, 1), :]
-    rows = lax.broadcasted_iota(jnp.int32, near_cols.shape, 0)
-    slot_ids = lax.broadcasted_iota(jnp.int32, near_cols.shape, 1)
-    by_col, by_task = near_cols[...], near_slots[...]
-    tile = (rows // pad) * (slot_count // 2) * row_count + rows % pad
-    last_code = 4 * near_hi.shape[0] - 1
-    coded = jnp.zeros(near_cols.shape, jnp.int32)
+    block_total = row_count * grid_size
+    first_row = row_count * (grid_place - 1)
+    rows = lax.broadcasted_iota(jnp.int32, cols.shape, 1)
+    slot_ids = lax.broadcasted_iota(jnp.int32, cols.shape, 0)
+    place = rows - first_row
+    place = jnp.where(place < 0, place + block_total, place)
+    place = jnp.where(place >= block_total, place - block_total, place)
+    tile = (place // row_count) * (slot_count // 2) * row_count + place % row_count
+    by_col, by_task = cols[...], slots[...]
+    coded = jnp.zeros(cols.shape, jnp.int32)
     for t in range(slot_count):
         coded += jnp.where(
-            by_task[:, t : t + 1] == slot_ids, 4 * (tile + (t // 2) * row_count) + t % 2 - 2, 0
+            by_task[t : t + 1] == slot_ids, 4 * (tile + (t // 2) * row_count) + t % 2 - 2, 0
         )
     for i in range(row_count):
-        mine = near_cols[pl.ds(pad + i, 1), :]
-        found = jnp.full(near_cols.shape, 2, jnp.int32)
+        mine = jnp.sum(
+            jnp.where(rows == row_count * grid_place + i, by_col, 0), axis=1, keepdims=True
+        )
+        found = jnp.full(cols.shape, 2, jnp.int32)
         for n in range(slot_count):
-            found += jnp.where(by_col[:, n : n + 1] == mine, coded[:, n : n + 1], 0)
-        codes_vmem[:, i * slot_count : (i + 1) * slot_count] = jnp.clip(found, 0, last_code)
+            found += jnp.where(by_col[n : n + 1] == mine, coded[n : n + 1], 0)
+        codes_vmem[i * slot_count : (i + 1) * slot_count, : cols.shape[1]] = jnp.clip(
+            found, 0, 4 * near_hi.shape[0] - 1
+        )
     to_smem = pltpu.make_async_copy(codes_vmem, codes, meta_sem.at[4])
     to_smem.start()
     convert(1, rep)
@@ -182,17 +184,9 @@
     lane_half = lax.broadcasted_iota(jnp.int32, (size, size), 1) // half
     nothing = jnp.zeros((size, size), jnp.bfloat16)
 
-    first_row = row_count * (grid_place - 1)
-    block_total = row_count * grid_size
-
-    def near_place(i, s, in_task_order):
+    def left_col(i, s, in_task_order):
         row = row_count * grid_place + i
-        slot = slots_smem[row, s] if in_task_order else s
-        place = cols_smem[row, slot] - first_row
-        place = jnp.where(place < 0, place + block_total, place)
-        place = jnp.where(place >= block_total, place - block_total, place)
-        place = jnp.clip(place, 0, 3 * row_count - 1)
-        return place + (pad - row_count) * (place // row_count)
+        return cols_smem[slots_smem[s, row] if in_task_order else s, row]
 
     def products(places, i, pair, lhs):
         total = jnp.zeros((half, 2 * size), jnp.float32)
@@ -201,7 +195,7 @@
             for t in (s, s + 1):
                 high_row, low_row = [], []
                 for m in range(2):
-                    code = codes[places[t], i * slot_count + 2 * pair + m]
+                    code = codes[i * slot_count + 2 * pair + m, places[t]]
                     tile = code // 4
                     keep = lane_half == code % 4
                     high_row.append(jnp.where(keep, near_hi[tile], nothing))
@@ -231,7 +225,7 @@
 
     @pl.loop(0, row_count)
     def _(i):
-        places = [near_place(i, s, True) for s in range(slot_count)]
+        places = [left_col(i, s, True) for s in range(slot_count)]
         lhs = left_operand([left[t // 2, i, t % 2] for t in range(slot_count)])
         for pair in range(slot_count // 2):
             square[side, i, pair] = products(places, i, pair, lhs)
@@ -249,7 +243,7 @@
     @pl.loop(0, row_count)
     def _(i):
         square_copy(i).wait_recv()
-        places = [near_place(i, s, False) for s in range(slot_count)]
+        places = [left_col(i, s, False) for s in range(slot_count)]
         tiles = []
         for pair in range(slot_count // 2):
             tiles.extend(swap(square[0, i, pair], square[1, i, pair]))
@@ -282,8 +276,9 @@
 def local(grid_size, rep_size, task_blocks, block_cols, task_slot):
     row_count, slots_here, size, _ = task_blocks.shape
     pairs = rep_size
-    pad = -(-row_count // 8) * 8
-    slot_count = block_cols.shape[1]
+    block_cols, task_slot = block_cols.T, task_slot.T
+    slot_count, block_total = block_cols.shape
+    lanes = -(-block_total // 128) * 128
     i32 = jnp.int32
     half = size // 2
     f32, bf16 = jnp.float32, jnp.bfloat16
@@ -302,10 +297,8 @@
             pltpu.VMEM(block_cols.shape, i32),
             pltpu.SMEM(block_cols.shape, i32),
             pltpu.SMEM(block_cols.shape, i32),
-            pltpu.VMEM((3 * pad, slot_count), i32),
-            pltpu.VMEM((3 * pad, slot_count), i32),
-            pltpu.VMEM((3 * pad, 128), i32),
-            pltpu.SMEM((3 * pad, 128), i32),
+            pltpu.VMEM((row_count * slot_count, lanes), i32),
+            pltpu.SMEM((row_count * slot_count, lanes), i32),
             pltpu.VMEM((row_count, slots_here, size, size), f32),
             pltpu.VMEM((row_count, size, size), f32),
             pltpu.VMEM((rep_size, row_count, slots_here, half, size), f32),

time: 75.1 us -> 72.9 us (0.971)
  local copies, waits for them, and re-layouts: 4.1 us -> 2.06 us
    unnamed x5 -> x1, local copies, waits for them, and re-layouts: 4.1 us -> 2.06 us
where the time goes in v3:
time: 72.9 us; the launch traced here: 72.8 us
  Pallas kernels  70.7 us (97%)
  local copies, waits for them, and re-layouts  2.06 us (3%)
    pallas_call x1, Pallas kernels, local(): pl.pallas_call(functools.partial(kernel, grid_size), out_shape=jax.ShapeD...  70.7 us
    unnamed x1, local copies, waits for them, and re-layouts  2.06 us

profile of v3, /device:TPU:0, one launch (start us, length us, event | category | flops | bytes accessed | tf_op | source)
XLA Modules:
  0.0 72.8 jit_solution(17728854975664850594)
XLA Ops:
  0.0 70.7 %shard_map.37 = f32[6,2,128,128]{3,2,1,0:T(8,128)} custom-call(f32[6,2,128,128]{3,2,1,0:T(8,128)} %task_ref.1, s32[8,24]{1,0:T(8,128)} %bitcast.2, s32[8,24]{1,0:T(8,128)} %bitcast.3), custom_call_target="tpu_custom_call" | custom-call | tf_op jit(solution)/shard_map/pallas_call | solution.py:286
  70.7 2.1 %copy.5 = f32[6,2,128,128]{3,2,1,0:T(8,128)} copy(f32[6,2,128,128]{3,2,1,0:T(8,128)} %shard_map.37) | data formatting | bytes 1572864

commit v4 on v3

--- a/solution.py
+++ b/solution.py
@@ -15,7 +15,7 @@
     cols, slots, cols_smem, slots_smem, codes_vmem, codes,
     own, stage, left, near, near_hi, near_lo, square, out_stage, landed,
     task_sem, meta_sem, z_send, z_recv, x_send, x_recv, s_send, s_recv,
-    l_send, l_recv, q_send, q_recv, o_send, o_recv,
+    l_send, l_recv, q_send, q_recv, o_send, o_recv, store_sem,
 ):
     row_count, _, size, _ = own.shape
     half = size // 2
@@ -255,19 +255,24 @@
             out_copy(i, n, peer).start()
         landed[side, i, pl.ds(pl.multiple_of(part * half, half), half), :] = out_stage[i, rep]
 
+    for copy in z_own + z_ctr + s_copies + lefts:
+        copy.wait_send()
+
+    def store(i):
+        return pltpu.make_async_copy(own.at[i], out_ref.at[i], store_sem.at[i])
+
     @pl.loop(0, row_count)
     def _(i):
         for n, peer in enumerate(peers):
             out_copy(i, n, peer).wait_recv()
         first, second = swap(landed[0, i], landed[1, i])
-        out_ref[i, 0] = first
-        out_ref[i, 1] = second
-
-    for copy in z_own + z_ctr + s_copies + lefts:
-        copy.wait_send()
-
-    @pl.loop(0, row_count)
-    def _(i):
+        own[i, 0] = first
+        own[i, 1] = second
+        store(i).start()
+
+    @pl.loop(0, row_count)
+    def _(i):
+        store(i).wait()
         square_copy(i).wait_send()
         for n, peer in enumerate(peers):
             out_copy(i, n, peer).wait_send()
@@ -291,7 +296,7 @@
             pl.BlockSpec(memory_space=pltpu.HBM),
             pl.BlockSpec(memory_space=pltpu.HBM),
         ],
-        out_specs=pl.BlockSpec(memory_space=pltpu.VMEM),
+        out_specs=pl.BlockSpec(memory_space=pltpu.HBM),
         scratch_shapes=[
             pltpu.VMEM(block_cols.shape, i32),
             pltpu.VMEM(block_cols.shape, i32),
@@ -310,7 +315,7 @@
             pltpu.VMEM((2, row_count, size, size), f32),
             dma, dma((5,)), dma((4,)), dma((4,)), dma, dma, dma((6,)), dma((6,)),
             dma((3,)), dma((3,)), dma((row_count,)), dma((row_count,)),
-            dma((3, row_count)), dma((3, row_count)),
+            dma((3, row_count)), dma((3, row_count)), dma((row_count,)),
         ],
         compiler_params=pltpu.CompilerParams(
             collective_id=0, has_side_effects=True, vmem_limit_bytes=62 * 1024 * 1024

time: 72.9 us -> 72.7 us (level)
  no operation moved by 1% of the time
where the time goes in v4:
time: 72.7 us; the launch traced here: 72.5 us
  Pallas kernels  70.4 us (97%)
  local copies, waits for them, and re-layouts  2.06 us (3%)
    pallas_call x1, Pallas kernels, local(): pl.pallas_call(functools.partial(kernel, grid_size), out_shape=jax.ShapeD...  70.4 us
    unnamed x1, local copies, waits for them, and re-layouts  2.06 us

profile of v4, /device:TPU:0, one launch (start us, length us, event | category | flops | bytes accessed | tf_op | source)
XLA Modules:
  0.0 72.5 jit_solution(1617902191337936539)
XLA Ops:
  0.0 70.4 %shard_map.37 = f32[6,2,128,128]{3,2,1,0:T(8,128)} custom-call(f32[6,2,128,128]{3,2,1,0:T(8,128)} %task_ref.1, s32[8,24]{1,0:T(8,128)} %bitcast.2, s32[8,24]{1,0:T(8,128)} %bitcast.3), custom_call_target="tpu_custom_call" | custom-call | tf_op jit(solution)/shard_map/pallas_call | solution.py:291
  70.4 2.1 %copy.5 = f32[6,2,128,128]{3,2,1,0:T(8,128)} copy(f32[6,2,128,128]{3,2,1,0:T(8,128)} %shard_map.37) | data formatting | bytes 1572864
